TPU v7x, 256 devices: a whole 4x4x8 slice. The times are simulated.
256 devices in a mesh: cfg: 2 (over core), seq: 16 (over x, z_hi), dp: 8 (over y, z_lo).
Axes of the slice: x: 4, y: 4, z: 8 (z_hi: 4, z_lo: 2; z = z_hi * 2 + z_lo), core: 2. Of those that a mesh axis runs over, the one named last changes fastest.
Arguments:
- image_projections: bfloat16 [2, 16, 2048, 6144], P('cfg', 'dp', 'seq'), may hold values from -8 to 8
- text_projections: bfloat16 [2, 16, 512, 4096], P('cfg', 'dp', 'seq'), may hold values from -6 to 6
- output_weight: bfloat16 [2048, 3072], P('seq', 'dp'), may hold values from -0.125 to 0.125
- image_state: bfloat16 [2, 16, 2048, 3072], P('cfg', 'dp', 'seq'), may hold values from -6 to 6
- modulation: bfloat16 [2, 16, 3, 3072], P('cfg', 'dp'), may hold values from -4 to 4
- final_weight: bfloat16 [3072, 64], replicated, may hold values from -0.109375 to 0.109375
- latent: float32 [16, 2048, 64], P('dp', 'seq'), may hold values from -6 to 6
- next_latent: float32 [16, 2048, 64], P('dp', 'seq'), may hold values from -8 to 8
- timestep: float32 [16], P('dp'), may hold values from 0.3 to 0.8
- rewards: float32 [16], P('dp'), may hold values from -5 to 5
- group_index: int32 [16], P('dp'), may hold values from 0 to 7, as said below
Outputs:
- grad_final_weight: float32 [3072, 64], P('dp')
- log_prob: float32 [16], P('dp')
Inputs may be any that keep to these rules, and one draw needn't show every extreme that they name: `group_index`: each of the 8 prompts has exactly 2 rollouts; rollout 0 shares its prompt with one of the last 2 rollouts.
All inputs are finite; a program needn't handle non-finite values.
Results may differ from a plain program's by a relative error of at most 0.00053.
Values may be sent and summed in bfloat16 or wider, within the bound.
No kernel may reach another device: no remote copies, remote signals or barrier semaphores. Data moves between devices by JAX's collectives and lax.ppermute only.
A program may use at most 64 MiB of HBM per device.

v0:
```python
import math

import jax
import jax.numpy as jnp
from jax import lax
from jax.sharding import PartitionSpec as P

C = 64
HD = 128
GROUP_SIZE = 2


cfg_scale = 4.5
noise_level = 0.7
step_width = 0.02
norm_eps = 1e-06


def swapped(value, axis, distance):
    mask = 2**distance
    pairs = [(source, source ^ mask) for source in range(lax.axis_size(axis))]
    return lax.ppermute(value, axis, pairs)


def attend_block(query, key_rows, value_rows):
    scores = jnp.einsum("qd,kd->qk", query, key_rows, preferred_element_type=jnp.float32) * (
        1.0 / math.sqrt(HD)
    )
    highest = jnp.max(scores, axis=1, keepdims=True)
    powered = jnp.exp(scores - highest)
    weights = (powered / jnp.sum(powered, axis=1, keepdims=True)).astype(jnp.bfloat16)
    return jnp.dot(weights, value_rows, preferred_element_type=jnp.float32).astype(jnp.bfloat16)


def modulate(mixed_rows, row_sums, squares, mods, width_all):
    center = row_sums / width_all
    square = squares / width_all
    normed = (mixed_rows - center) * lax.rsqrt(square - center * center + norm_eps)
    scale_rows = mods[:, 2][:, None, :].astype(jnp.float32)
    shift_rows = mods[:, 1][:, None, :].astype(jnp.float32)
    return (normed * (1.0 + scale_rows) + shift_rows).astype(jnp.bfloat16)


def step_terms(conditional, unconditional, latent, next_latent, timestep, advantage, rollouts):
    guided = unconditional + cfg_scale * (conditional - unconditional)
    moment = timestep[:, None, None]
    spread = noise_level * jnp.sqrt(moment / (1.0 - moment))
    drift_gain = 1.0 + spread * spread * (1.0 - moment) / (2.0 * moment)
    step_mean = (
        latent * (1.0 - spread * spread / (2.0 * moment) * step_width)
        - guided * drift_gain * step_width
    )
    deviation = spread * math.sqrt(step_width)
    residue = next_latent - step_mean
    density = (
        -residue * residue / (2.0 * deviation * deviation)
        - jnp.log(deviation)
        - 0.5 * math.log(2.0 * math.pi)
    )
    slopes = (
        advantage[:, None, None]
        / (rollouts * C)
        * drift_gain
        * step_width
        / (deviation * deviation)
        * residue
    )
    return (density, slopes)


def per_device(
    image_projections,
    text_projections,
    output_weight,
    image_state,
    modulation,
    final_weight,
    latent,
    next_latent,
    timestep,
    rewards,
    group_index,
):
    seq_count = lax.axis_size("seq")
    data_count = lax.axis_size("dp")
    per_dev = image_projections.shape[1]
    image_count = image_projections.shape[2]
    text_count = text_projections.shape[2]
    head_width = image_projections.shape[3] // 3
    width_all = image_state.shape[3]
    head_slab = head_width // seq_count
    rollouts = per_dev * data_count
    image_split = image_projections.reshape(per_dev, image_count, 3, seq_count, head_slab)
    text_split = text_projections.reshape(per_dev, text_count, 2, seq_count, head_slab)
    image_part = lax.all_to_all(image_split, "seq", split_axis=3, concat_axis=1, tiled=True)
    text_part = lax.all_to_all(text_split, "seq", split_axis=3, concat_axis=1, tiled=True)
    item_count = image_part.shape[0]
    full_rows = image_part.shape[1]
    heads_here = head_slab // HD

    def split_heads(tensor):
        row_count = tensor.shape[1]
        tensor = tensor.reshape(item_count, row_count, heads_here, HD).transpose(0, 2, 1, 3)
        return tensor.reshape(item_count * heads_here, row_count, HD)

    queries = split_heads(image_part[:, :, 0, 0])
    key_rows = split_heads(jnp.concatenate([image_part[:, :, 1, 0], text_part[:, :, 0, 0]], 1))
    value_rows = split_heads(jnp.concatenate([image_part[:, :, 2, 0], text_part[:, :, 1, 0]], 1))
    block_rows = min(512, full_rows)

    def per_head(triple):
        head_queries, head_keys, head_values = triple

        def per_block(block_queries):
            return attend_block(block_queries, head_keys, head_values)

        outputs = lax.map(per_block, head_queries.reshape(full_rows // block_rows, block_rows, HD))
        return outputs.reshape(full_rows, HD)

    mixed_heads = lax.map(per_head, (queries, key_rows, value_rows))
    mixed_heads = mixed_heads.reshape(item_count, heads_here, full_rows, HD).transpose(0, 2, 1, 3)
    mixed_heads = mixed_heads.reshape(item_count, seq_count, full_rows // seq_count, 1, head_slab)
    returned = lax.all_to_all(mixed_heads, "seq", split_axis=1, concat_axis=3, tiled=True)
    attention = returned.reshape(item_count, full_rows // seq_count, seq_count * head_slab)
    group_count = rollouts // GROUP_SIZE
    member = (group_index[:, None] == jnp.arange(group_count, dtype=jnp.int32)[None, :]).astype(
        jnp.float32
    )
    totals = lax.psum(jnp.sum(member * rewards[:, None], axis=0), "dp")
    advantage = rewards - jnp.sum(member * totals[None, :], axis=1) / GROUP_SIZE
    state_local = image_state[0]
    mods_local = modulation[0]
    rows_weight = lax.all_gather(output_weight, "dp", axis=1, tiled=True)
    flat_attention = attention.reshape(-1, head_width)
    projected = jnp.dot(
        flat_attention,
        lax.all_gather(rows_weight, "seq", axis=0, tiled=True),
        preferred_element_type=jnp.float32,
    )
    projected = projected.reshape(per_dev, image_count, width_all)
    mixed_rows = (
        state_local.astype(jnp.float32)
        + mods_local[:, 0][:, None, :].astype(jnp.float32) * projected
    )
    row_sums = jnp.sum(mixed_rows, axis=2, keepdims=True)
    squares = jnp.sum(mixed_rows * mixed_rows, axis=2, keepdims=True)
    hidden = modulate(mixed_rows, row_sums, squares, mods_local, width_all)
    hidden_flat = hidden.reshape(-1, width_all)
    velocity = jnp.dot(hidden_flat, final_weight, preferred_element_type=jnp.float32)
    velocity = velocity.reshape(per_dev, image_count, -1)
    index_cfg = lax.axis_index("cfg")
    partner = swapped(velocity, "cfg", 0)
    is_first = index_cfg == 0
    cond_velocity = jnp.where(is_first, velocity, partner)
    unconditional = jnp.where(is_first, partner, velocity)
    density, slopes = step_terms(
        cond_velocity, unconditional, latent, next_latent, timestep, advantage, rollouts
    )
    factor = jnp.where(is_first, cfg_scale, 1.0 - cfg_scale)
    own_slopes = (factor * slopes).astype(jnp.bfloat16)
    log_sum = lax.psum(jnp.sum(density, axis=(1, 2)), "seq")
    own_slopes, log_prob = (own_slopes, log_sum / (seq_count * image_count * C))
    partial_grad = jnp.einsum(
        "nd,nc->dc",
        hidden_flat,
        own_slopes.reshape(-1, own_slopes.shape[2]),
        preferred_element_type=jnp.float32,
    )
    col_count = width_all // data_count
    full_grad = lax.psum(partial_grad, ("cfg", "seq", "dp"))
    gradient = lax.dynamic_slice_in_dim(full_grad, lax.axis_index("dp") * col_count, col_count, 0)
    return (gradient, log_prob)


def solution(mesh):
    in_specs = (
        P("cfg", "dp", "seq", None),
        P("cfg", "dp", "seq", None),
        P("seq", "dp"),
        P("cfg", "dp", "seq", None),
        P("cfg", "dp", None, None),
        P(),
        P("dp", "seq", None),
        P("dp", "seq", None),
        P("dp"),
        P("dp"),
        P("dp"),
    )
    out_specs = (P("dp", None), P("dp"))
    return jax.shard_map(
        per_device, mesh=mesh, in_specs=in_specs, out_specs=out_specs, check_vma=False
    )
```

profile of v0, /device:TPU:1, one launch (start us, length us, event | category | flops | bytes accessed | tf_op | source)
XLA Modules:
  0.0 583.0 jit_solution(1591787033663537476)
XLA Ops:
  9.4 11.6 %all-to-all-start.1 = ((bf16[2,32,2,16,128]{4,1,0,2,3:T(8,128)(2,1)}), bf16[2,32,2,16,128]{4,1,0,2,3:T(8,128)(2,1)}, u32[]{:S(2)}, u32[]{:S(2)}) async-start(bf16[2,32,2,16,128]{4,1,0,2,3:T(8,128)(2,1)} %copy.29), calls=%async_computation.1 | async-start | bytes 1048576 | tf_op jit(solution)/shard_map/all_to_all | solution.py:96
  21.1 37.2 %all_gather.6 = bf16[128,3072]{1,0:T(8,128)(2,1)} all-gather(bf16[128,384]{1,0:T(8,128)(2,1)S(1)} %copy-done.5), channel_id=1, replica_groups=mesh['cfg'=2,'seq'=16,'dp'=8] {'dp'}, dimensions={1}, use_global_device_ids=true | all-gather | bytes 884736 | tf_op jit(solution)/shard_map/all_gather | solution.py:133
  58.3 3.5 copy.26
  61.8 2.8 copy.27
  64.7 9.2 %all-to-all-start = ((bf16[2,128,3,16,128]{4,1,0,2,3:T(8,128)(2,1)}), bf16[2,128,3,16,128]{4,1,0,2,3:T(8,128)(2,1)S(1)}, u32[]{:S(2)}, u32[]{:S(2)}) async-start(bf16[2,128,3,16,128]{4,1,0,2,3:T(8,128)(2,1)} %copy.27), calls=%async_computation | async-start | bytes 6291456 | tf_op jit(solution)/shard_map/all_to_all | solution.py:95
  75.8 95.9 %all-to-all-done = bf16[2,128,3,16,128]{4,1,0,2,3:T(8,128)(2,1)S(1)} async-done(((bf16[2,128,3,16,128]{4,1,0,2,3:T(8,128)(2,1)}), bf16[2,128,3,16,128]{4,1,0,2,3:T(8,128)(2,1)S(1)}, u32[]{:S(2)}, u32[]{:S(2)}) %all-to-all-start) | async-done | bytes 3145760 | tf_op jit(solution)/shard_map/all_to_all | solution.py:95
  173.3 1.3 pad_maximum_fusion
  174.6 35.7 %while.21 = (s32[]{:T(128)}, bf16[2,2048,128]{2,1,0:T(8,128)(2,1)}, bf16[2,2048,128]{2,1,0:T(8,128)(2,1)}, bf16[2,2560,128]{2,1,0:T(8,128)(2,1)S(1)}, bf16[2,256...) while((s32[]{:T(128)}, bf16[2,2048,128]{2,1,0:T(8,128)(2,1)}, bf16[2,2048,128]{2,1,0:T(8,128)(2,1)}, ...), condition=%wide.region_5.6_spmd, body=%wide.region_0.5_spmd.sunk | while | flops 680328192 | bytes 22031580 | solution.py:120
  176.9 13.7 %while.22 = (s32[]{:T(128)}, bf16[4,512,128]{2,1,0:T(8,128)(2,1)}, bf16[4,512,128]{2,1,0:T(8,128)(2,1)S(1)}, bf16[2560,128]{1,0:T(8,128)(2,1)S(1)}, bf16[2560,128]{1,0:T(8,128)(2,1)S(1)}, /*index=5*/s32[]{:T(128)}) while((s32[]{:T(128)}, bf16[4,512,128]{2,1,0:T(8,128)(2,1)}, bf16[4,512,128]{2,1,0:T(8,128)(2,1)S(1)}, ...), condition=%wide.region_4.4_spmd, body=%wide.region_1.3_spmd.sunk | while | flops 680328192 | bytes 17312328 | solution.py:117
  178.7 1.6 fusion.46
  182.1 1.7 fusion.46
  185.5 1.6 fusion.46
  188.9 1.6 fusion.46
  190.6 1.9 bitcast_dynamic-update-slice_fusion.2
  194.8 13.7 %while.22 = (s32[]{:T(128)}, bf16[4,512,128]{2,1,0:T(8,128)(2,1)}, bf16[4,512,128]{2,1,0:T(8,128)(2,1)S(1)}, bf16[2560,128]{1,0:T(8,128)(2,1)S(1)}, bf16[2560,128]{1,0:T(8,128)(2,1)S(1)}, /*index=5*/s32[]{:T(128)}) while((s32[]{:T(128)}, bf16[4,512,128]{2,1,0:T(8,128)(2,1)}, bf16[4,512,128]{2,1,0:T(8,128)(2,1)S(1)}, ...), condition=%wide.region_4.4_spmd, body=%wide.region_1.3_spmd.sunk | while | flops 680328192 | bytes 17312328 | solution.py:117
  196.6 1.6 fusion.46
  200.0 1.7 fusion.46
  203.4 1.6 fusion.46
  206.8 1.6 fusion.46
  208.5 1.9 bitcast_dynamic-update-slice_fusion.2
  210.4 2.4 copy.33
  212.8 6.0 %all-to-all-start.2 = ((bf16[2,16,128,1,128]{4,2,0,3,1:T(8,128)(2,1)}), bf16[2,16,128,1,128]{4,2,0,3,1:T(8,128)(2,1)S(1)}, u32[]{:S(2)}, u32[]{:S(2)}) async-start(bf16[2,16,128,1,128]{4,2,0,3,1:T(8,128)(2,1)} %copy.33), calls=%async_computation.2 | async-start | bytes 2097152 | tf_op jit(solution)/shard_map/all_to_all | solution.py:123
  219.0 66.7 %psum.21 = f32[8]{0:T(128)S(1)} all-reduce(f32[8]{0:T(128)S(1)} %select_reduce_fusion.1), channel_id=1, replica_groups=mesh['cfg'=2,'seq'=16,'dp'=8] {'dp'}, use_global_device_ids=true, to_apply=%region_9.10 | all-reduce | flops 8 | bytes 64 | tf_op jit(solution)/shard_map/psum | solution.py:129
  288.9 1.3 dot_general.17
  290.2 17.3 %all-gather.2.cloned.1.call-done = bf16[2048,3072]{1,0:T(8,128)(2,1)} async-done(((bf16[128,3072]{1,0:T(8,128)(2,1)}), bf16[2048,3072]{1,0:T(8,128)(2,1)}) %all-gather.2.cloned.1.call-update) | async-done | bytes 12582928 | tf_op jit(solution)/shard_map/all_gather | solution.py:137
  307.5 9.1 %fusion.30 = (f32[2,128]{1,0:T(2,128)S(1)}, f32[2,128]{1,0:T(2,128)S(1)}, f32[2,128,3072]{2,1,0:T(8,128)S(1)}) fusion(bf16[2,128,2048]{2,1,0:T(8,128)(2,1)} %dot_general.17, bf16[2048,3072]{1,0:T(8,128)(2,1)} %all-gather.2.cloned.1.call-done, f32[2,3072]{1,0:T(2,128)} %get-tuple-element.95, bf16[1,2,128,3072]{3,2,1,0:T(8,128)(2,1)} %param.18), kind=kOutput, calls=%fused_computation.63 | convolution fusion | flops 3225943552 | bytes 18376704 | tf_op jit(solution)/shard_map/dot_general | solution.py:135
  316.6 1.4 fusion.16
  319.9 1.7 fusion.21
  321.6 2.4 convolution_bitcast_fusion
  324.0 36.2 %psum.23 = f32[2]{0:T(128)S(1)} all-reduce(f32[2]{0:T(128)S(1)} %copy-done.7), channel_id=1, replica_groups=mesh['cfg'=2,'seq'=16,'dp'=8] {'seq'}, use_global_device_ids=true, to_apply=%region_13.14 | all-reduce | flops 2 | bytes 16 | tf_op jit(solution)/shard_map/psum | solution.py:161
  360.7 213.9 %all-reduce.2.cloned.1.call-done = f32[3072,64]{0,1:T(8,128)} async-done(((f32[3072,64]{0,1:T(8,128)}), f32[3072,64]{0,1:T(8,128)}) %all-reduce.2.cloned.1.call-update) | async-done | bytes 786448 | tf_op jit(solution)/shard_map/psum | solution.py:170
  574.6 1.5 constant_dynamic-slice_fusion.1
  (76 shorter events, 30.3 us)
Async XLA Ops:
  7.2 309.4 %copy-start = (bf16[3072,64]{0,1:T(8,128)(2,1)S(1)}, bf16[3072,64]{0,1:T(8,128)(2,1)}, u32[]{:S(2)}) copy-start(bf16[3072,64]{0,1:T(8,128)(2,1)} %param.20) | copy-start | bytes 1179652
  7.2 13.9 %copy-start.5 = (bf16[128,384]{1,0:T(8,128)(2,1)S(1)}, bf16[128,384]{1,0:T(8,128)(2,1)}, u32[]{:S(2)}) copy-start(bf16[128,384]{1,0:T(8,128)(2,1)} %param.17) | copy-start | bytes 294916
  9.4 55.2 %all-to-all-start.1 = ((bf16[2,32,2,16,128]{4,1,0,2,3:T(8,128)(2,1)}), bf16[2,32,2,16,128]{4,1,0,2,3:T(8,128)(2,1)}, u32[]{:S(2)}, u32[]{:S(2)}) async-start(bf16[2,32,2,16,128]{4,1,0,2,3:T(8,128)(2,1)} %copy.29), calls=%async_computation.1 | async-start | bytes 1048576 | tf_op jit(solution)/shard_map/all_to_all | solution.py:96
  21.1 286.4 %all-gather.2.cloned.1.call-start = ((), (), s32[]{:S(2)}) async-start(), calls=%async_computation.3 | async-start | bytes 13369344 | tf_op jit(solution)/shard_map/all_gather | solution.py:137
  64.7 107.1 %all-to-all-start = ((bf16[2,128,3,16,128]{4,1,0,2,3:T(8,128)(2,1)}), bf16[2,128,3,16,128]{4,1,0,2,3:T(8,128)(2,1)S(1)}, u32[]{:S(2)}, u32[]{:S(2)}) async-start(bf16[2,128,3,16,128]{4,1,0,2,3:T(8,128)(2,1)} %copy.27), calls=%async_computation | async-start | bytes 6291456 | tf_op jit(solution)/shard_map/all_to_all | solution.py:95
  172.1 1.2 copy-start.1
  172.1 1.2 copy-start.2
  210.4 8.5 %copy-start.8 = (f32[2]{0:T(128)S(1)}, f32[2]{0:T(128)}, u32[]{:S(2)}) copy-start(f32[2]{0:T(128)} %param.24) | copy-start | bytes 28
  210.4 8.5 %copy-start.14 = (s32[2]{0:T(128)S(1)}, s32[2]{0:T(128)}, u32[]{:S(2)}) copy-start(s32[2]{0:T(128)} %param.25) | copy-start | bytes 28
  210.4 76.1 %copy-start.10 = (f32[2]{0:T(128)S(1)}, f32[2]{0:T(128)}, u32[]{:S(2)}) copy-start(f32[2]{0:T(128)} %param.23) | copy-start | bytes 28
  210.4 76.6 %copy-start.6 = (bf16[1,2,3,3072]{3,1,2,0:T(2,128)(2,1)S(1)}, bf16[1,2,3,3072]{3,1,2,0:T(2,128)(2,1)}, u32[]{:S(2)}) copy-start(bf16[1,2,3,3072]{3,1,2,0:T(2,128)(2,1)} %param.19) | copy-start | bytes 110596
  212.8 75.4 %all-to-all-start.2 = ((bf16[2,16,128,1,128]{4,2,0,3,1:T(8,128)(2,1)}), bf16[2,16,128,1,128]{4,2,0,3,1:T(8,128)(2,1)S(1)}, u32[]{:S(2)}, u32[]{:S(2)}) async-start(bf16[2,16,128,1,128]{4,2,0,3,1:T(8,128)(2,1)} %copy.33), calls=%async_computation.2 | async-start | bytes 2097152 | tf_op jit(solution)/shard_map/all_to_all | solution.py:123
  218.8 355.8 %all-reduce.2.cloned.1.call-start = ((), (), s32[]{:S(2)}) async-start(), calls=%async_computation.4 | async-start | bytes 1572864 | tf_op jit(solution)/shard_map/psum | solution.py:170
  307.5 9.1 %copy-start.3 = (f32[2,3072]{1,0:T(2,128)S(1)}, f32[2,3072]{1,0:T(2,128)}, u32[]{:S(2)}) copy-start(f32[2,3072]{1,0:T(2,128)} %add_bitcast_fusion) | copy-start | bytes 73732
  307.5 9.2 %copy-start.4 = (f32[2,3072]{1,0:T(2,128)S(1)}, f32[2,3072]{1,0:T(2,128)}, u32[]{:S(2)}) copy-start(f32[2,3072]{1,0:T(2,128)} %get-tuple-element.94) | copy-start | bytes 73732
  316.5 2.1 copy-start.9
  316.5 2.1 copy-start.11
  316.5 2.1 copy-start.12
  316.6 2.1 copy-start.13
  318.0 1.9 collective-permute-start
  321.6 2.4 copy-start.7
Sparse Core Ops, SparseCore 0:
  58.4 248.9 all-gather.1
  324.1 250.4 all-reduce.1
where the time goes:
time: 585 us; the launch traced here: 583 us
  waiting for transfers between devices  328 us (56%)
  blocking collectives  140 us (24%)
  matrix products  33.4 us (6%)
  starting transfers between devices  27.6 us (5%)
  local copies, waits for them, and re-layouts  26.4 us (5%)
  between operations  14.3 us (2%)
  other arithmetic  13.4 us (2%)
    psum x1, waiting for transfers between devices, per_device(): full_grad = lax.psum(partial_grad, ('cfg', 'seq', 'dp'))  214 us
    all_to_all x1, waiting for transfers between devices, per_device(): lax.all_to_all(image_split, 'seq', split_axis=3, concat_axis=1, tiled=True)  95.9 us
    psum x1, blocking collectives, per_device(): totals = lax.psum(jnp.sum(member * rewards[:, None], axis=0), 'dp')  66.7 us
    all_gather x1, blocking collectives, per_device(): rows_weight = lax.all_gather(output_weight, 'dp', axis=1, tiled=True)  37.2 us
    psum x1, blocking collectives, per_device(): log_sum = lax.psum(jnp.sum(density, axis=(1, 2)), 'seq')  36.2 us
    all_gather x1, waiting for transfers between devices, per_device(): lax.all_gather(rows_weight, 'seq', axis=0, tiled=True)  17.3 us
    dot_general x8, matrix products, attend_block(): jnp.dot(weights, value_rows, preferred_element_type=jnp.float32)  13.2 us
  transfers between devices with their start and end apart: 6, of which 4 were waited for; matrix products, arithmetic and copies ran while one was open for 9% of the time, Pallas kernels for 0%

commit v1 on v0

v1 whole, which is shorter than its diff:
```python
import math

import jax
import jax.numpy as jnp
from jax import lax
from jax.experimental import pallas as pl
from jax.experimental.pallas import tpu as pltpu
from jax.sharding import PartitionSpec as P

C = 64
HD = 128
GROUP_SIZE = 2

cfg_scale = 4.5
noise_level = 0.7
step_width = 0.02
norm_eps = 1e-06

X, ZH, Y, ZL = 4, 4, 4, 2
VMEM_BYTES = 56 * 1024 * 1024


def from_x(value, d):
    pairs = [(((x + d) % X) * ZH + z, x * ZH + z) for x in range(X) for z in range(ZH)]
    return lax.ppermute(value, "seq", pairs)


def from_zh(value, d):
    pairs = [(x * ZH + (z + d) % ZH, x * ZH + z) for x in range(X) for z in range(ZH)]
    return lax.ppermute(value, "seq", pairs)


def from_y(value, d):
    pairs = [(((y + d) % Y) * ZL + z, y * ZL + z) for y in range(Y) for z in range(ZL)]
    return lax.ppermute(value, "dp", pairs)


def from_zl(value):
    pairs = [(y * ZL + 1 - z, y * ZL + z) for y in range(Y) for z in range(ZL)]
    return lax.ppermute(value, "dp", pairs)


def from_cfg(value):
    return lax.ppermute(value, "cfg", [(0, 1), (1, 0)])


def ring_sum(value, fetch):
    first, second, third = (fetch(value, d) for d in (1, 2, 3))
    return (value + second) + (first + third)


def pack_kernel(q_ref, k_ref, v_ref, kt_ref, vt_ref, out_ref):
    rows, text = q_ref.shape[2], kt_ref.shape[2]
    for h in range(out_ref.shape[0]):
        cols = slice(h * HD, (h + 1) * HD)
        out_ref[h, 0:rows, :] = q_ref[0, 0, :, cols]
        out_ref[h, rows : 2 * rows, :] = k_ref[0, 0, :, cols]
        out_ref[h, 2 * rows : 2 * rows + text, :] = kt_ref[0, 0, :, cols]
        out_ref[h, 2 * rows + text : 3 * rows + text, :] = v_ref[0, 0, :, cols]
        out_ref[h, 3 * rows + text : 3 * rows + 2 * text, :] = vt_ref[0, 0, :, cols]


def pack(image_projections, text_projections, r):
    rows, text = image_projections.shape[2], text_projections.shape[2]
    heads = image_projections.shape[3] // (3 * HD)
    per = 4
    steps = heads // per
    total = 3 * rows + 2 * text

    def spec(count, part):
        return pl.BlockSpec((1, 1, count, per * HD), lambda h: (0, r, 0, part * steps + h))

    return pl.pallas_call(
        pack_kernel,
        grid=(steps,),
        in_specs=[spec(rows, 0), spec(rows, 1), spec(rows, 2), spec(text, 0), spec(text, 1)],
        out_specs=pl.BlockSpec((per, total, HD), lambda h: (h, 0, 0)),
        out_shape=jax.ShapeDtypeStruct((heads, total, HD), jnp.bfloat16),
        compiler_params=pltpu.CompilerParams(vmem_limit_bytes=32 * 1024 * 1024),
        cost_estimate=pl.CostEstimate(
            flops=0, bytes_accessed=2 * heads * total * HD * 2, transcendentals=0
        ),
        name=f"pack{r}",
    )(image_projections, image_projections, image_projections, text_projections, text_projections)


def attention_kernel(parts_ref, out_ref, keys, values):
    peers = parts_ref.shape[0]
    per_step, rows = out_ref.shape[0], out_ref.shape[1]
    kv_rows = keys.shape[0] // peers
    step = pl.program_id(0)

    @pl.when(step == 0)
    def _():
        ones = jnp.ones((kv_rows, HD), jnp.bfloat16)
        for s in range(peers):
            at = slice(s * kv_rows, (s + 1) * kv_rows)
            keys[at, :] = parts_ref[s, rows : rows + kv_rows, :]
            values[at, 0:HD] = parts_ref[s, rows + kv_rows : rows + 2 * kv_rows, :]
            values[at, HD : 2 * HD] = ones

    factor = math.log2(math.e) / math.sqrt(HD)
    queries = parts_ref[pl.ds(step * per_step, per_step), 0:rows, :].reshape(per_step * rows, HD)
    scores = lax.dot_general(
        queries, keys[...], (((1,), (1,)), ((), ())), preferred_element_type=jnp.float32
    )
    highest = jnp.max(scores, axis=1, keepdims=True)
    powered = jnp.exp2((scores - highest) * factor).astype(jnp.bfloat16)
    sums = jnp.dot(powered, values[...], preferred_element_type=jnp.float32)
    result = sums[:, 0:HD] / sums[:, HD : HD + 1]
    out_ref[...] = result.astype(jnp.bfloat16).reshape(per_step, rows, HD)


def attention(parts, rows, per_step=2):
    peers, total, _ = parts.shape
    kv_rows = (total - rows) // 2
    return pl.pallas_call(
        attention_kernel,
        grid=(peers // per_step,),
        in_specs=[pl.BlockSpec((peers, total, HD), lambda i: (0, 0, 0))],
        out_specs=pl.BlockSpec((per_step, rows, HD), lambda i: (i, 0, 0)),
        out_shape=jax.ShapeDtypeStruct((peers, rows, HD), jnp.bfloat16),
        scratch_shapes=[
            pltpu.VMEM((peers * kv_rows, HD), jnp.bfloat16),
            pltpu.VMEM((peers * kv_rows, 2 * HD), jnp.bfloat16),
        ],
        compiler_params=pltpu.CompilerParams(vmem_limit_bytes=VMEM_BYTES),
        cost_estimate=pl.CostEstimate(
            flops=8 * peers * rows * peers * kv_rows * HD,
            bytes_accessed=2 * peers * total * HD,
            transcendentals=peers * rows * peers * kv_rows,
        ),
        name="attention",
    )(parts)


def hidden_kernel(place, heads_ref, state_ref, mods_ref, final_ref, *rest):
    pieces, (hidden_ref, velocity_ref, flat, mixed, weights, sems) = rest[:10], rest[10:]
    x_at, zh_at, y_at, c_at = place[0], place[1], place[2], place[3]
    heads = heads_ref.shape[0]
    depth = heads * HD
    width = weights.shape[2]
    half = heads // 2
    spans = ((0, 0, heads), (1, 0, heads), (3, 0, heads), (2, 0, half), (2, half, half))
    copies = []
    for core in range(2):
        for n, (turn, first, count) in enumerate(spans):
            copy = pltpu.make_async_copy(
                pieces[core * 5 + n],
                weights.at[core * 4 + turn, pl.ds(first * HD, count * HD)],
                sems.at[core * 5 + n],
            )
            copy.start()
            copies.append(copy)
    for i in range(X):
        for j in range(ZH):
            head = lax.rem(x_at + i, X) * ZH + lax.rem(zh_at + j, ZH)
            k = i * ZH + j
            flat[:, k * HD : (k + 1) * HD] = heads_ref[head]
    rows = flat.shape[0]
    row_sum = jnp.zeros((rows, 1), jnp.float32)
    square_sum = jnp.zeros((rows, 1), jnp.float32)
    for core in range(2):
        core_at = c_at if core == 0 else 1 - c_at
        for turn, needed in ((0, (0,)), (1, (1,)), (3, (2,)), (2, (3, 4))):
            for n in needed:
                copies[core * 5 + n].wait()
            at = pl.ds(pl.multiple_of((lax.rem(y_at + turn, Y) * ZL + core_at) * width, 128), width)
            projected = jnp.dot(
                flat[...], weights[core * 4 + turn], preferred_element_type=jnp.float32
            )
            gate = mods_ref[0, 0:1, at].astype(jnp.float32)
            block = state_ref[0, 0, :, at].astype(jnp.float32) + gate * projected
            mixed[:, at] = block
            row_sum = row_sum + jnp.sum(block, axis=1, keepdims=True)
            square_sum = square_sum + jnp.sum(block * block, axis=1, keepdims=True)
    width_all = mixed.shape[1]
    center = row_sum / width_all
    square = square_sum / width_all
    inverse = lax.rsqrt(square - center * center + norm_eps)
    scale = 1.0 + mods_ref[0, 2:3, :].astype(jnp.float32)
    shift = mods_ref[0, 1:2, :].astype(jnp.float32)
    hidden = ((mixed[...] - center) * inverse * scale + shift).astype(jnp.bfloat16)
    hidden_ref[...] = hidden
    velocity_ref[...] = jnp.dot(hidden, final_ref[...], preferred_element_type=jnp.float32)


def hidden_rows(place, heads_part, image_state, modulation, final_weight, pieces, r):
    heads, rows, _ = heads_part.shape
    width_all = image_state.shape[3]
    width = pieces[0].shape[1]
    whole = pl.BlockSpec(memory_space=pltpu.VMEM)
    return pl.pallas_call(
        hidden_kernel,
        grid=(1,),
        in_specs=[
            pl.BlockSpec(memory_space=pltpu.SMEM),
            pl.BlockSpec((heads, rows, HD), lambda i: (0, 0, 0)),
            pl.BlockSpec((1, 1, rows, width_all), lambda i: (0, r, 0, 0)),
            pl.BlockSpec((1, 3, width_all), lambda i: (r, 0, 0)),
            pl.BlockSpec((width_all, C), lambda i: (0, 0)),
        ]
        + [pl.BlockSpec(memory_space=pl.ANY)] * 10,
        out_specs=[
            pl.BlockSpec((rows, width_all), lambda i: (0, 0)),
            pl.BlockSpec((rows, C), lambda i: (0, 0)),
        ],
        out_shape=[
            jax.ShapeDtypeStruct((rows, width_all), jnp.bfloat16),
            jax.ShapeDtypeStruct((rows, C), jnp.float32),
        ],
        scratch_shapes=[
            pltpu.VMEM((rows, heads * HD), jnp.bfloat16),
            pltpu.VMEM((rows, width_all), jnp.float32),
            pltpu.VMEM((8, heads * HD, width), jnp.bfloat16),
            pltpu.SemaphoreType.DMA((10,)),
        ],
        compiler_params=pltpu.CompilerParams(vmem_limit_bytes=VMEM_BYTES),
        cost_estimate=pl.CostEstimate(
            flops=2 * rows * heads * HD * width_all,
            bytes_accessed=2 * heads * HD * width_all,
            transcendentals=0,
        ),
        name=f"hidden{r}",
    )(place, heads_part, image_state, modulation, final_weight, *pieces)


def gather_weight(output_weight, zl_at, c_at):
    depth, width = output_weight.shape
    mine = jnp.where(zl_at == c_at, output_weight, from_zl(output_weight))
    column = jnp.concatenate([mine] + [from_zh(mine, d) for d in range(1, ZH)], axis=0)
    plane = jnp.concatenate([column] + [from_x(column, d) for d in range(1, X)], axis=0)
    cut = plane.shape[0] // 2
    ahead = from_y(plane, 1)
    behind = from_y(plane, -1)
    far_first = from_y(ahead[:cut], 1)
    far_second = from_y(behind[cut:], -1)
    own = [plane, ahead, behind, far_first, far_second]
    return own + [from_cfg(piece) for piece in own]


def step_terms(conditional, unconditional, latent, next_latent, timestep, advantage, rollouts):
    guided = unconditional + cfg_scale * (conditional - unconditional)
    moment = timestep[:, None, None]
    spread = noise_level * jnp.sqrt(moment / (1.0 - moment))
    drift_gain = 1.0 + spread * spread * (1.0 - moment) / (2.0 * moment)
    step_mean = (
        latent * (1.0 - spread * spread / (2.0 * moment) * step_width)
        - guided * drift_gain * step_width
    )
    deviation = spread * math.sqrt(step_width)
    residue = next_latent - step_mean
    density = (
        -residue * residue / (2.0 * deviation * deviation)
        - jnp.log(deviation)
        - 0.5 * math.log(2.0 * math.pi)
    )
    slopes = (
        advantage[:, None, None]
        / (rollouts * C)
        * drift_gain
        * step_width
        / (deviation * deviation)
        * residue
    )
    return (density, slopes)


def exchange(send):
    return lax.all_to_all(send, "seq", split_axis=0, concat_axis=0, tiled=True)


def per_device(
    image_projections,
    text_projections,
    output_weight,
    image_state,
    modulation,
    final_weight,
    latent,
    next_latent,
    timestep,
    rewards,
    group_index,
):
    seq_count = lax.axis_size("seq")
    data_count = lax.axis_size("dp")
    per_dev = image_projections.shape[1]
    image_count = image_projections.shape[2]
    width_all = image_state.shape[3]
    rollouts = per_dev * data_count
    seq_at, dp_at, c_at = lax.axis_index("seq"), lax.axis_index("dp"), lax.axis_index("cfg")
    x_at, zh_at, y_at, zl_at = seq_at // ZH, seq_at % ZH, dp_at // ZL, dp_at % ZL
    place = jnp.stack([x_at, zh_at, y_at, c_at]).astype(jnp.int32)

    parts = [
        exchange(pack(image_projections, text_projections, r)) for r in range(per_dev)
    ]
    pieces = gather_weight(output_weight, zl_at, c_at)

    group_count = rollouts // GROUP_SIZE
    member = (group_index[:, None] == jnp.arange(group_count, dtype=jnp.int32)[None, :]).astype(
        jnp.float32
    )
    totals = jnp.sum(member * rewards[:, None], axis=0)
    totals = totals + from_zl(totals)
    totals = ring_sum(totals, from_y)
    advantage = rewards - jnp.sum(member * totals[None, :], axis=1) / GROUP_SIZE

    returned = [exchange(attention(part, image_count)) for part in parts]
    mods_local = modulation[0]
    rows = [
        hidden_rows(place, returned[r], image_state, mods_local, final_weight, pieces, r)
        for r in range(per_dev)
    ]
    hidden = jnp.concatenate([row[0] for row in rows], axis=0)
    velocity = jnp.stack([row[1] for row in rows])
    partner = from_cfg(velocity)
    is_first = c_at == 0
    cond_velocity = jnp.where(is_first, velocity, partner)
    unconditional = jnp.where(is_first, partner, velocity)
    density, slopes = step_terms(
        cond_velocity, unconditional, latent, next_latent, timestep, advantage, rollouts
    )
    factor = jnp.where(is_first, cfg_scale, 1.0 - cfg_scale)
    own_slopes = (factor * slopes).astype(jnp.bfloat16)
    log_sums = jnp.sum(density, axis=(1, 2))

    partial = lax.dot_general(
        own_slopes.reshape(-1, C), hidden, (((0,), (0,)), ((), ())), preferred_element_type=jnp.float32
    )
    col_count = width_all // data_count
    half = C // 2
    partial = partial.reshape(2, half, data_count, col_count).transpose(0, 2, 1, 3)
    kept = jnp.where(is_first, partial[0], partial[1]) + from_cfg(
        jnp.where(is_first, partial[1], partial[0])
    )
    spread_parts = lax.all_to_all(kept, "dp", split_axis=0, concat_axis=0, tiled=True)
    share = jnp.sum(spread_parts, axis=0)
    share = share.reshape(half * col_count // 128, 128)
    tail = jnp.concatenate(
        [jnp.broadcast_to(log_sums[:, None], (per_dev, 128)), jnp.zeros((8 - per_dev, 128), jnp.float32)]
    )
    share = jnp.concatenate([share, tail], axis=0)
    share = ring_sum(ring_sum(share, from_zh), from_x)
    log_sum = share[-8 : per_dev - 8, 0]
    log_prob = log_sum / (seq_count * image_count * C)
    share = share[:-8].reshape(half, col_count)
    other = from_cfg(share)
    first = jnp.where(is_first, share, other)
    second = jnp.where(is_first, other, share)
    gradient = jnp.concatenate([first, second], axis=0).T
    return (gradient, log_prob)


def solution(mesh):
    in_specs = (
        P("cfg", "dp", "seq", None),
        P("cfg", "dp", "seq", None),
        P("seq", "dp"),
        P("cfg", "dp", "seq", None),
        P("cfg", "dp", None, None),
        P(),
        P("dp", "seq", None),
        P("dp", "seq", None),
        P("dp"),
        P("dp"),
        P("dp"),
    )
    out_specs = (P("dp", None), P("dp"))
    return jax.shard_map(
        per_device, mesh=mesh, in_specs=in_specs, out_specs=out_specs, check_vma=False
    )
```

time: 585 us -> 297 us (0.51)
  waiting for transfers between devices: 328 us -> 130 us
  blocking collectives: 140 us -> 0 us
  starting transfers between devices: 27.6 us -> 84.1 us
  Pallas kernels: 0 us -> 50.8 us
  matrix products: 33.4 us -> 0.59 us
  between operations: 14.3 us -> 1.02 us
  local copies, waits for them, and re-layouts: 26.4 us -> 18.3 us
    psum x1 -> x0, waiting for transfers between devices: 214 us -> none  [per_device(): full_grad = lax.psum(partial_grad, ('cfg', 'seq', 'dp'))]
    psum x2 -> x0, blocking collectives: 103 us -> none  [the longest x1 66.7 us: per_device(): totals = lax.psum(jnp.sum(member * rewards[:, None], axis=0), 'dp')]
    ppermute x1 -> x29, waiting for transfers between devices: 0.65 us -> 83.2 us  [the longest x2 52.4 us: from_zl(): return lax.ppermute(value, 'dp', pairs)]
    pallas_call x0 -> x6, Pallas kernels: none -> 50.8 us  [the longest x2 32.6 us: attention(): pl.pallas_call(attention_kernel, grid=(peers // per_step,), in_specs=[pl....]
    all_to_all x3 -> x5, waiting for transfers between devices: 95.9 us -> 47.2 us  [the longest x4 39 us: exchange(): return lax.all_to_all(send, 'seq', split_axis=0, concat_axis=0, tiled=True)]
    ppermute x1 -> x29, starting transfers between devices: 0.68 us -> 44.7 us  [the longest x6 12.9 us: from_zh(): return lax.ppermute(value, 'seq', pairs)]
    all_gather x1 -> x0, blocking collectives: 37.2 us -> none  [per_device(): rows_weight = lax.all_gather(output_weight, 'dp', axis=1, tiled=True)]
    dot_general x19 -> x1, matrix products: 33.4 us -> 0.59 us  [per_device(): lax.dot_general(own_slopes.reshape(-1, C), hidden, (((0,), (0,)), ((), ()...]
  transfers between devices with their start and end apart: 6 -> 34, of which waited for: 4 -> 18; matrix products, arithmetic and copies ran while one was open for 9% -> 6% of each run, Pallas kernels for 0% -> 14%
where the time goes in v1:
time: 297 us; the launch traced here: 296 us
  waiting for transfers between devices  130 us (44%)
  starting transfers between devices  84.1 us (28%)
  Pallas kernels  50.8 us (17%)
  local copies, waits for them, and re-layouts  18.3 us (6%)
  other arithmetic  10.5 us (4%)
    ppermute x2, waiting for transfers between devices, from_zl(): return lax.ppermute(value, 'dp', pairs)  52.4 us
    all_to_all x4, waiting for transfers between devices, exchange(): return lax.all_to_all(send, 'seq', split_axis=0, concat_axis=0, tiled=True)  39 us
    all_to_all x4, starting transfers between devices, exchange(): return lax.all_to_all(send, 'seq', split_axis=0, concat_axis=0, tiled=True)  35.4 us
    pallas_call x2, Pallas kernels, attention(): pl.pallas_call(attention_kernel, grid=(peers // per_step,), in_specs=[pl....  32.6 us
    ppermute x6, waiting for transfers between devices, from_x(): return lax.ppermute(value, 'seq', pairs)  17.9 us
    pallas_call x2, Pallas kernels, hidden_rows(): pl.pallas_call(hidden_kernel, grid=(1,), in_specs=[pl.BlockSpec(memory_sp...  17 us
    unnamed x39, local copies, waits for them, and re-layouts  14.6 us
    ppermute x6, starting transfers between devices, from_zh(): return lax.ppermute(value, 'seq', pairs)  12.9 us
  transfers between devices with their start and end apart: 34, of which 18 were waited for; matrix products, arithmetic and copies ran while one was open for 6% of the time, Pallas kernels for 14%

profile of v1, /device:TPU:1, one launch (start us, length us, event | category | flops | bytes accessed | tf_op | source)
XLA Modules:
  0.0 295.7 jit_solution(12756216421929006942)
XLA Ops:
  0.6 1.9 copy-done
  5.4 11.9 %all-to-all-start = ((bf16[16,448,128]{2,1,0:T(8,128)(2,1)}), bf16[16,448,128]{2,1,0:T(8,128)(2,1)}, u32[]{:S(2)}, u32[]{:S(2)}) async-start(bf16[16,448,128]{2,1,0:T(8,128)(2,1)} %copy-done.5), calls=%async_computation | async-start | bytes 3670016 | tf_op jit(solution)/shard_map/all_to_all | solution.py:270
  20.2 39.0 %all-to-all-done.parts_ref = bf16[16,448,128]{2,1,0:T(8,128)(2,1)} async-done(((bf16[16,448,128]{2,1,0:T(8,128)(2,1)}), bf16[16,448,128]{2,1,0:T(8,128)(2,1)}, u32[]{:S(2)}, u32[]{:S(2)}) %all-to-all-start) | async-done | bytes 1835040 | tf_op jit(solution)/shard_map/all_to_all | solution.py:270
  59.2 7.8 %all-to-all-start.2 = ((bf16[16,448,128]{2,1,0:T(8,128)(2,1)}), bf16[16,448,128]{2,1,0:T(8,128)(2,1)}, u32[]{:S(2)}, u32[]{:S(2)}) async-start(bf16[16,448,128]{2,1,0:T(8,128)(2,1)} %copy-done.4), calls=%async_computation.2 | async-start | bytes 3670016 | tf_op jit(solution)/shard_map/all_to_all | solution.py:270
  67.0 1.9 collective-permute-start.4
  69.0 42.8 %collective-permute-done.4 = bf16[128,384]{1,0:T(8,128)(2,1)S(1)} collective-permute-done((bf16[128,384]{1,0:T(8,128)(2,1)S(1)}, bf16[128,384]{1,0:T(8,128)(2,1)S(1)}, u32[]{:S(2)}, u32[]{:S(2)}) %collective-permute-start.4) | collective-permute-done | bytes 98336 | tf_op jit(solution)/shard_map/ppermute | solution.py:40
  112.4 2.8 collective-permute-start.5
  116.1 2.4 collective-permute-start.7
  119.4 3.4 %collective-permute-done.6 = bf16[128,384]{1,0:T(8,128)(2,1)S(1)} collective-permute-done((bf16[128,384]{1,0:T(8,128)(2,1)S(1)}, bf16[128,384]{1,0:T(8,128)(2,1)S(1)}, u32[]{:S(2)}, u32[]{:S(2)}) %collective-permute-start.6) | collective-permute-done | bytes 98336 | tf_op jit(solution)/shard_map/ppermute | solution.py:30
  122.8 2.9 collective-permute-done.7
  125.7 3.0 %collective-permute-start.8 = (bf16[512,384]{1,0:T(8,128)(2,1)S(1)}, bf16[512,384]{1,0:T(8,128)(2,1)S(1)}, u32[]{:S(2)}, u32[]{:S(2)}) collective-permute-start(bf16[512,384]{1,0:T(8,128)(2,1)S(1)} %pad_maximum_fusion), channel_id=1, source_target_pairs={{32,0},{40,8},{48,16},{56,24},{64,32},{72,40},{80,48},{88,56},{96,... | collective-permute-start | bytes 1179656 | tf_op jit(solution)/shard_map/ppermute | solution.py:25
  128.7 3.0 %collective-permute-start.9 = (bf16[512,384]{1,0:T(8,128)(2,1)S(1)}, bf16[512,384]{1,0:T(8,128)(2,1)S(1)}, u32[]{:S(2)}, u32[]{:S(2)}) collective-permute-start(bf16[512,384]{1,0:T(8,128)(2,1)S(1)} %pad_maximum_fusion), channel_id=1, source_target_pairs={{64,0},{72,8},{80,16},{88,24},{96,32},{104,40},{112,48},{120,56},{... | collective-permute-start | bytes 1179656 | tf_op jit(solution)/shard_map/ppermute | solution.py:25
  134.4 2.2 collective-permute-done.8
  137.4 2.3 collective-permute-done.9
  140.5 9.2 %collective-permute-done.10 = bf16[512,384]{1,0:T(8,128)(2,1)S(1)} collective-permute-done((bf16[512,384]{1,0:T(8,128)(2,1)S(1)}, bf16[512,384]{1,0:T(8,128)(2,1)S(1)}, u32[]{:S(2)}, u32[]{:S(2)}) %collective-permute-start.10) | collective-permute-done | bytes 393248 | tf_op jit(solution)/shard_map/ppermute | solution.py:25
  150.5 2.7 collective-permute-start.11
  153.2 16.3 %attention.2 = bf16[16,128,128]{2,1,0:T(8,128)(2,1)} custom-call(bf16[16,448,128]{2,1,0:T(8,128)(2,1)} %all-to-all-done.parts_ref), custom_call_target="tpu_custom_call" | custom-call | flops 5368709120 | bytes 1835008 | tf_op jit(solution)/shard_map/attention/pallas_call | solution.py:117
  169.5 6.5 %all-to-all-start.1 = ((bf16[16,128,128]{2,1,0:T(8,128)(2,1)}), bf16[16,128,128]{2,1,0:T(8,128)(2,1)}, u32[]{:S(2)}, u32[]{:S(2)}) async-start(bf16[16,128,128]{2,1,0:T(8,128)(2,1)} %attention.2), calls=%async_computation.1 | async-start | bytes 1048576 | tf_op jit(solution)/shard_map/all_to_all | solution.py:270
  177.1 9.7 %collective-permute-done = f32[8]{0:T(128)S(1)} collective-permute-done((f32[8]{0:T(128)S(1)}, f32[8]{0:T(128)S(1)}, u32[]{:S(2)}, u32[]{:S(2)}) %collective-permute-start) | collective-permute-done | bytes 64 | tf_op jit(solution)/shard_map/ppermute | solution.py:40
  190.0 3.2 %collective-permute-start.15 = (bf16[2048,384]{1,0:T(8,128)(2,1)}, bf16[2048,384]{1,0:T(8,128)(2,1)}, u32[]{:S(2)}, u32[]{:S(2)}) collective-permute-start(bf16[2048,384]{1,0:T(8,128)(2,1)} %constant_dynamic-update-slice_fusion.rest_0_), channel_id=1, source_target_pairs={{0,128},{128,0},{1,129},{129,1},{2,130},{130,2},{3,131},{131,3},{4... | collective-permute-start | bytes 4718600 | tf_op jit(solution)/shard_map/ppermute | solution.py:44
  194.2 2.0 collective-permute-start.13
  197.8 16.3 %attention.3 = bf16[16,128,128]{2,1,0:T(8,128)(2,1)} custom-call(bf16[16,448,128]{2,1,0:T(8,128)(2,1)} %all-to-all-done.2.parts_ref), custom_call_target="tpu_custom_call" | custom-call | flops 5368709120 | bytes 1835008 | tf_op jit(solution)/shard_map/attention/pallas_call | solution.py:117
  214.1 9.2 %all-to-all-start.3 = ((bf16[16,128,128]{2,1,0:T(8,128)(2,1)}), bf16[16,128,128]{2,1,0:T(8,128)(2,1)}, u32[]{:S(2)}, u32[]{:S(2)}) async-start(bf16[16,128,128]{2,1,0:T(8,128)(2,1)} %attention.3), calls=%async_computation.3 | async-start | bytes 1048576 | tf_op jit(solution)/shard_map/all_to_all | solution.py:270
  232.3 8.5 %hidden0.1 = (bf16[128,3072]{1,0:T(8,128)(2,1)}, f32[128,64]{1,0:T(8,128)}) custom-call(s32[4]{0:T(128)} %pad_add_fusion.place, bf16[16,128,128]{2,1,0:T(8,128)(2,1)} %all-to-all-done.1.heads_ref, bf16[1,2,128,3072]{3,2,1,0:T(8,128)(2,1)} %state_ref.3, bf16[2,3,3072]{2,1,0:T(4,128)(2,1)} %bitcast.33, bf16[3072,64]{1,0:T(8,128)(2,1)} %copy.44.final_ref, ...), custom_call_target="tpu_custom_call" | custom-call | flops 1610612736 | bytes 12582912 | tf_op jit(solution)/shard_map/hidden0/pallas_call | solution.py:193
  240.8 8.5 %hidden1.1 = (bf16[128,3072]{1,0:T(8,128)(2,1)}, f32[128,64]{1,0:T(8,128)}) custom-call(s32[4]{0:T(128)} %pad_add_fusion.place, bf16[16,128,128]{2,1,0:T(8,128)(2,1)} %all-to-all-done.3.heads_ref, bf16[1,2,128,3072]{3,2,1,0:T(8,128)(2,1)} %state_ref.3, bf16[2,3,3072]{2,1,0:T(4,128)(2,1)} %bitcast.34, bf16[3072,64]{1,0:T(8,128)(2,1)} %copy.44.final_ref, ...), custom_call_target="tpu_custom_call" | custom-call | flops 1610612736 | bytes 12582912 | tf_op jit(solution)/shard_map/hidden1/pallas_call | solution.py:193
  258.8 4.1 %all-to-all-start.4 = ((f32[8,32,384]{2,1,0:T(8,128)}), f32[8,32,384]{2,1,0:T(8,128)S(1)}, u32[]{:S(2)}, u32[]{:S(2)}) async-start(f32[8,32,384]{2,1,0:T(8,128)} %bitcast_add_fusion), calls=%async_computation.4 | async-start | bytes 786432 | tf_op jit(solution)/shard_map/all_to_all | solution.py:338
  263.1 8.1 %all-to-all-done.4 = f32[8,32,384]{2,1,0:T(8,128)S(1)} async-done(((f32[8,32,384]{2,1,0:T(8,128)}), f32[8,32,384]{2,1,0:T(8,128)S(1)}, u32[]{:S(2)}, u32[]{:S(2)}) %all-to-all-start.4) | async-done | bytes 393248 | tf_op jit(solution)/shard_map/all_to_all | solution.py:338
  271.3 4.4 %collective-permute-start.22 = (f32[104,128]{1,0:T(8,128)S(1)}, f32[104,128]{1,0:T(8,128)S(1)}, u32[]{:S(2)}, u32[]{:S(2)}) collective-permute-start(f32[104,128]{1,0:T(8,128)S(1)} %maximum_maximum_fusion), channel_id=1, source_target_pairs={{16,0},{24,8},{0,16},{8,24},{48,32},{56,40},{32,48},{40,56},{80,64... | collective-permute-start | bytes 159752 | tf_op jit(solution)/shard_map/ppermute | solution.py:30
  278.4 2.9 collective-permute-done.23
  282.0 2.6 collective-permute-start.25
  287.5 2.7 collective-permute-done.27
  290.3 3.9 %collective-permute-start.28 = (f32[32,384]{1,0:T(8,128)S(1)}, f32[32,384]{1,0:T(8,128)S(1)}, u32[]{:S(2)}, u32[]{:S(2)}) collective-permute-start(f32[32,384]{1,0:T(8,128)S(1)} %reshape.54), channel_id=1, source_target_pairs={{0,128},{128,0},{1,129},{129,1},{2,130},{130,2},{3,131},{131,3},{4... | collective-permute-start | bytes 147464 | tf_op jit(solution)/shard_map/ppermute | solution.py:44
  (115 shorter events, 46.6 us)
Async XLA Ops:
  5.4 53.8 %all-to-all-start = ((bf16[16,448,128]{2,1,0:T(8,128)(2,1)}), bf16[16,448,128]{2,1,0:T(8,128)(2,1)}, u32[]{:S(2)}, u32[]{:S(2)}) async-start(bf16[16,448,128]{2,1,0:T(8,128)(2,1)} %copy-done.5), calls=%async_computation | async-start | bytes 3670016 | tf_op jit(solution)/shard_map/all_to_all | solution.py:270
  59.2 110.2 %all-to-all-start.2 = ((bf16[16,448,128]{2,1,0:T(8,128)(2,1)}), bf16[16,448,128]{2,1,0:T(8,128)(2,1)}, u32[]{:S(2)}, u32[]{:S(2)}) async-start(bf16[16,448,128]{2,1,0:T(8,128)(2,1)} %copy-done.4), calls=%async_computation.2 | async-start | bytes 3670016 | tf_op jit(solution)/shard_map/all_to_all | solution.py:270
  67.0 44.7 %collective-permute-start.4 = (bf16[128,384]{1,0:T(8,128)(2,1)S(1)}, bf16[128,384]{1,0:T(8,128)(2,1)S(1)}, u32[]{:S(2)}, u32[]{:S(2)}) collective-permute-start(bf16[128,384]{1,0:T(8,128)(2,1)S(1)} %copy-done.12), channel_id=1, source_target_pairs={{1,0},{0,1},{3,2},{2,3},{5,4},{4,5},{7,6},{6,7},{9,8},{8,9},{11,10... | collective-permute-start | bytes 294920 | tf_op jit(solution)/shard_map/ppermute | solution.py:40
  112.4 7.0 %collective-permute-start.5 = (bf16[128,384]{1,0:T(8,128)(2,1)S(1)}, bf16[128,384]{1,0:T(8,128)(2,1)S(1)}, u32[]{:S(2)}, u32[]{:S(2)}) collective-permute-start(bf16[128,384]{1,0:T(8,128)(2,1)S(1)} %get-tuple-element.17), channel_id=1, source_target_pairs={{8,0},{16,8},{24,16},{0,24},{40,32},{48,40},{56,48},{32,56},{72,64... | collective-permute-start | bytes 294920 | tf_op jit(solution)/shard_map/ppermute | solution.py:30
  115.2 7.6 %collective-permute-start.6 = (bf16[128,384]{1,0:T(8,128)(2,1)S(1)}, bf16[128,384]{1,0:T(8,128)(2,1)S(1)}, u32[]{:S(2)}, u32[]{:S(2)}) collective-permute-start(bf16[128,384]{1,0:T(8,128)(2,1)S(1)} %get-tuple-element.17), channel_id=1, source_target_pairs={{16,0},{24,8},{0,16},{8,24},{48,32},{56,40},{32,48},{40,56},{80,64... | collective-permute-start | bytes 294920 | tf_op jit(solution)/shard_map/ppermute | solution.py:30
  116.1 9.5 %collective-permute-start.7 = (bf16[128,384]{1,0:T(8,128)(2,1)S(1)}, bf16[128,384]{1,0:T(8,128)(2,1)S(1)}, u32[]{:S(2)}, u32[]{:S(2)}) collective-permute-start(bf16[128,384]{1,0:T(8,128)(2,1)S(1)} %get-tuple-element.17), channel_id=1, source_target_pairs={{24,0},{0,8},{8,16},{16,24},{56,32},{32,40},{40,48},{48,56},{88,64... | collective-permute-start | bytes 294920 | tf_op jit(solution)/shard_map/ppermute | solution.py:30
  125.7 10.9 %collective-permute-start.8 = (bf16[512,384]{1,0:T(8,128)(2,1)S(1)}, bf16[512,384]{1,0:T(8,128)(2,1)S(1)}, u32[]{:S(2)}, u32[]{:S(2)}) collective-permute-start(bf16[512,384]{1,0:T(8,128)(2,1)S(1)} %pad_maximum_fusion), channel_id=1, source_target_pairs={{32,0},{40,8},{48,16},{56,24},{64,32},{72,40},{80,48},{88,56},{96,... | collective-permute-start | bytes 1179656 | tf_op jit(solution)/shard_map/ppermute | solution.py:25
  128.7 11.0 %collective-permute-start.9 = (bf16[512,384]{1,0:T(8,128)(2,1)S(1)}, bf16[512,384]{1,0:T(8,128)(2,1)S(1)}, u32[]{:S(2)}, u32[]{:S(2)}) collective-permute-start(bf16[512,384]{1,0:T(8,128)(2,1)S(1)} %pad_maximum_fusion), channel_id=1, source_target_pairs={{64,0},{72,8},{80,16},{88,24},{96,32},{104,40},{112,48},{120,56},{... | collective-permute-start | bytes 1179656 | tf_op jit(solution)/shard_map/ppermute | solution.py:25
  131.7 18.0 %collective-permute-start.10 = (bf16[512,384]{1,0:T(8,128)(2,1)S(1)}, bf16[512,384]{1,0:T(8,128)(2,1)S(1)}, u32[]{:S(2)}, u32[]{:S(2)}) collective-permute-start(bf16[512,384]{1,0:T(8,128)(2,1)S(1)} %pad_maximum_fusion), channel_id=1, source_target_pairs={{96,0},{104,8},{112,16},{120,24},{0,32},{8,40},{16,48},{24,56},{32... | collective-permute-start | bytes 1179656 | tf_op jit(solution)/shard_map/ppermute | solution.py:25
  150.5 39.5 %collective-permute-start.11 = (bf16[2048,384]{1,0:T(8,128)(2,1)}, bf16[2048,384]{1,0:T(8,128)(2,1)S(1)}, u32[]{:S(2)}, u32[]{:S(2)}) collective-permute-start(bf16[2048,384]{1,0:T(8,128)(2,1)} %constant_dynamic-update-slice_fusion.rest_0_), channel_id=1, source_target_pairs={{2,0},{3,1},{4,2},{5,3},{6,4},{7,5},{0,6},{1,7},{10,8},{11,9},{12,... | collective-permute-start | bytes 4718600 | tf_op jit(solution)/shard_map/ppermute | solution.py:35
  153.2 41.0 %collective-permute-start.12 = (bf16[2048,384]{1,0:T(8,128)(2,1)}, bf16[2048,384]{1,0:T(8,128)(2,1)S(1)}, u32[]{:S(2)}, u32[]{:S(2)}) collective-permute-start(bf16[2048,384]{1,0:T(8,128)(2,1)} %constant_dynamic-update-slice_fusion.rest_0_), channel_id=1, source_target_pairs={{6,0},{7,1},{0,2},{1,3},{2,4},{3,5},{4,6},{5,7},{14,8},{15,9},{8,1... | collective-permute-start | bytes 4718600 | tf_op jit(solution)/shard_map/ppermute | solution.py:35
  169.5 44.7 %all-to-all-start.1 = ((bf16[16,128,128]{2,1,0:T(8,128)(2,1)}), bf16[16,128,128]{2,1,0:T(8,128)(2,1)}, u32[]{:S(2)}, u32[]{:S(2)}) async-start(bf16[16,128,128]{2,1,0:T(8,128)(2,1)} %attention.2), calls=%async_computation.1 | async-start | bytes 1048576 | tf_op jit(solution)/shard_map/all_to_all | solution.py:270
  176.1 10.7 %collective-permute-start = (f32[8]{0:T(128)S(1)}, f32[8]{0:T(128)S(1)}, u32[]{:S(2)}, u32[]{:S(2)}) collective-permute-start(f32[8]{0:T(128)S(1)} %select_reduce_fusion.1), channel_id=1, source_target_pairs={{1,0},{0,1},{3,2},{2,3},{5,4},{4,5},{7,6},{6,7},{9,8},{8,9},{11,10... | collective-permute-start | bytes 104 | tf_op jit(solution)/shard_map/ppermute | solution.py:40
  186.8 10.4 %collective-permute-start.1 = (f32[8]{0:T(128)S(1)}, f32[8]{0:T(128)S(1)}, u32[]{:S(2)}, u32[]{:S(2)}) collective-permute-start(f32[8]{0:T(128)S(1)} %add.50), channel_id=1, source_target_pairs={{4,0},{5,1},{6,2},{7,3},{0,4},{1,5},{2,6},{3,7},{12,8},{13,9},{14,... | collective-permute-start | bytes 104 | tf_op jit(solution)/shard_map/ppermute | solution.py:35
  188.4 8.8 %collective-permute-start.2 = (f32[8]{0:T(128)S(1)}, f32[8]{0:T(128)S(1)}, u32[]{:S(2)}, u32[]{:S(2)}) collective-permute-start(f32[8]{0:T(128)S(1)} %add.50), channel_id=1, source_target_pairs={{2,0},{3,1},{4,2},{5,3},{6,4},{7,5},{0,6},{1,7},{10,8},{11,9},{12,... | collective-permute-start | bytes 104 | tf_op jit(solution)/shard_map/ppermute | solution.py:35
  189.4 8.3 %collective-permute-start.3 = (f32[8]{0:T(128)S(1)}, f32[8]{0:T(128)S(1)}, u32[]{:S(2)}, u32[]{:S(2)}) collective-permute-start(f32[8]{0:T(128)S(1)} %add.50), channel_id=1, source_target_pairs={{6,0},{7,1},{0,2},{1,3},{2,4},{3,5},{4,6},{5,7},{14,8},{15,9},{8,1... | collective-permute-start | bytes 104 | tf_op jit(solution)/shard_map/ppermute | solution.py:35
  190.0 42.3 %collective-permute-start.15 = (bf16[2048,384]{1,0:T(8,128)(2,1)}, bf16[2048,384]{1,0:T(8,128)(2,1)}, u32[]{:S(2)}, u32[]{:S(2)}) collective-permute-start(bf16[2048,384]{1,0:T(8,128)(2,1)} %constant_dynamic-update-slice_fusion.rest_0_), channel_id=1, source_target_pairs={{0,128},{128,0},{1,129},{129,1},{2,130},{130,2},{3,131},{131,3},{4... | collective-permute-start | bytes 4718600 | tf_op jit(solution)/shard_map/ppermute | solution.py:44
  194.2 33.3 %collective-permute-start.13 = (bf16[1024,384]{1,0:T(8,128)(2,1)}, bf16[1024,384]{1,0:T(8,128)(2,1)}, u32[]{:S(2)}, u32[]{:S(2)}) collective-permute-start(bf16[1024,384]{1,0:T(8,128)(2,1)} %slice.26), channel_id=1, source_target_pairs={{2,0},{3,1},{4,2},{5,3},{6,4},{7,5},{0,6},{1,7},{10,8},{11,9},{12,... | collective-permute-start | bytes 2359304 | tf_op jit(solution)/shard_map/ppermute | solution.py:35
  197.2 31.1 %collective-permute-start.14 = (bf16[1024,384]{1,0:T(8,128)(2,1)}, bf16[1024,384]{1,0:T(8,128)(2,1)}, u32[]{:S(2)}, u32[]{:S(2)}) collective-permute-start(bf16[1024,384]{1,0:T(8,128)(2,1)} %slice.27), channel_id=1, source_target_pairs={{6,0},{7,1},{0,2},{1,3},{2,4},{3,5},{4,6},{5,7},{14,8},{15,9},{8,1... | collective-permute-start | bytes 2359304 | tf_op jit(solution)/shard_map/ppermute | solution.py:35
  197.2 35.1 %collective-permute-start.16 = (bf16[2048,384]{1,0:T(8,128)(2,1)S(1)}, bf16[2048,384]{1,0:T(8,128)(2,1)}, u32[]{:S(2)}, u32[]{:S(2)}) collective-permute-start(bf16[2048,384]{1,0:T(8,128)(2,1)S(1)} %collective-permute-done.11.rest_1_), channel_id=1, source_target_pairs={{0,128},{128,0},{1,129},{129,1},{2,130},{130,2},{3,131},{131,3},{4... | collective-permute-start | bytes 4718600 | tf_op jit(solution)/shard_map/ppermute | solution.py:44
  197.6 34.6 %collective-permute-start.17 = (bf16[2048,384]{1,0:T(8,128)(2,1)S(1)}, bf16[2048,384]{1,0:T(8,128)(2,1)}, u32[]{:S(2)}, u32[]{:S(2)}) collective-permute-start(bf16[2048,384]{1,0:T(8,128)(2,1)S(1)} %collective-permute-done.12.rest_2_), channel_id=1, source_target_pairs={{0,128},{128,0},{1,129},{129,1},{2,130},{130,2},{3,131},{131,3},{4... | collective-permute-start | bytes 4718600 | tf_op jit(solution)/shard_map/ppermute | solution.py:44
  214.1 26.7 %all-to-all-start.3 = ((bf16[16,128,128]{2,1,0:T(8,128)(2,1)}), bf16[16,128,128]{2,1,0:T(8,128)(2,1)}, u32[]{:S(2)}, u32[]{:S(2)}) async-start(bf16[16,128,128]{2,1,0:T(8,128)(2,1)} %attention.3), calls=%async_computation.3 | async-start | bytes 1048576 | tf_op jit(solution)/shard_map/all_to_all | solution.py:270
  227.5 4.7 %collective-permute-start.18 = (bf16[1024,384]{1,0:T(8,128)(2,1)}, bf16[1024,384]{1,0:T(8,128)(2,1)}, u32[]{:S(2)}, u32[]{:S(2)}) collective-permute-start(bf16[1024,384]{1,0:T(8,128)(2,1)} %collective-permute-done.13.rest_3_), channel_id=1, source_target_pairs={{0,128},{128,0},{1,129},{129,1},{2,130},{130,2},{3,131},{131,3},{4... | collective-permute-start | bytes 2359304 | tf_op jit(solution)/shard_map/ppermute | solution.py:44
  228.2 4.0 %collective-permute-start.19 = (bf16[1024,384]{1,0:T(8,128)(2,1)}, bf16[1024,384]{1,0:T(8,128)(2,1)}, u32[]{:S(2)}, u32[]{:S(2)}) collective-permute-start(bf16[1024,384]{1,0:T(8,128)(2,1)} %collective-permute-done.14.rest_4_), channel_id=1, source_target_pairs={{0,128},{128,0},{1,129},{129,1},{2,130},{130,2},{3,131},{131,3},{4... | collective-permute-start | bytes 2359304 | tf_op jit(solution)/shard_map/ppermute | solution.py:44
  250.9 3.2 %collective-permute-start.20 = (f32[2,128,64]{2,1,0:T(8,128)}, f32[2,128,64]{2,1,0:T(8,128)}, u32[]{:S(2)}, u32[]{:S(2)}) collective-permute-start(f32[2,128,64]{2,1,0:T(8,128)} %pad_maximum_fusion.1), channel_id=1, source_target_pairs={{0,128},{128,0},{1,129},{129,1},{2,130},{130,2},{3,131},{131,3},{4... | collective-permute-start | bytes 196616 | tf_op jit(solution)/shard_map/ppermute | solution.py:44
  258.8 12.4 %all-to-all-start.4 = ((f32[8,32,384]{2,1,0:T(8,128)}), f32[8,32,384]{2,1,0:T(8,128)S(1)}, u32[]{:S(2)}, u32[]{:S(2)}) async-start(f32[8,32,384]{2,1,0:T(8,128)} %bitcast_add_fusion), calls=%async_computation.4 | async-start | bytes 786432 | tf_op jit(solution)/shard_map/all_to_all | solution.py:338
  271.3 7.1 %collective-permute-start.22 = (f32[104,128]{1,0:T(8,128)S(1)}, f32[104,128]{1,0:T(8,128)S(1)}, u32[]{:S(2)}, u32[]{:S(2)}) collective-permute-start(f32[104,128]{1,0:T(8,128)S(1)} %maximum_maximum_fusion), channel_id=1, source_target_pairs={{16,0},{24,8},{0,16},{8,24},{48,32},{56,40},{32,48},{40,56},{80,64... | collective-permute-start | bytes 159752 | tf_op jit(solution)/shard_map/ppermute | solution.py:30
  275.8 5.6 %collective-permute-start.23 = (f32[104,128]{1,0:T(8,128)S(1)}, f32[104,128]{1,0:T(8,128)S(1)}, u32[]{:S(2)}, u32[]{:S(2)}) collective-permute-start(f32[104,128]{1,0:T(8,128)S(1)} %maximum_maximum_fusion), channel_id=1, source_target_pairs={{8,0},{16,8},{24,16},{0,24},{40,32},{48,40},{56,48},{32,56},{72,64... | collective-permute-start | bytes 159752 | tf_op jit(solution)/shard_map/ppermute | solution.py:30
  276.4 5.5 %collective-permute-start.24 = (f32[104,128]{1,0:T(8,128)S(1)}, f32[104,128]{1,0:T(8,128)S(1)}, u32[]{:S(2)}, u32[]{:S(2)}) collective-permute-start(f32[104,128]{1,0:T(8,128)S(1)} %maximum_maximum_fusion), channel_id=1, source_target_pairs={{24,0},{0,8},{8,16},{16,24},{56,32},{32,40},{40,48},{48,56},{88,64... | collective-permute-start | bytes 159752 | tf_op jit(solution)/shard_map/ppermute | solution.py:30
  282.0 4.6 %collective-permute-start.25 = (f32[104,128]{1,0:T(8,128)S(1)}, f32[104,128]{1,0:T(8,128)S(1)}, u32[]{:S(2)}, u32[]{:S(2)}) collective-permute-start(f32[104,128]{1,0:T(8,128)S(1)} %add_add_fusion.1), channel_id=1, source_target_pairs={{64,0},{72,8},{80,16},{88,24},{96,32},{104,40},{112,48},{120,56},{... | collective-permute-start | bytes 159752 | tf_op jit(solution)/shard_map/ppermute | solution.py:25
  285.4 4.8 %collective-permute-start.27 = (f32[104,128]{1,0:T(8,128)S(1)}, f32[104,128]{1,0:T(8,128)S(1)}, u32[]{:S(2)}, u32[]{:S(2)}) collective-permute-start(f32[104,128]{1,0:T(8,128)S(1)} %add_add_fusion.1), channel_id=1, source_target_pairs={{96,0},{104,8},{112,16},{120,24},{0,32},{8,40},{16,48},{24,56},{32... | collective-permute-start | bytes 159752 | tf_op jit(solution)/shard_map/ppermute | solution.py:25
  290.3 4.8 %collective-permute-start.28 = (f32[32,384]{1,0:T(8,128)S(1)}, f32[32,384]{1,0:T(8,128)S(1)}, u32[]{:S(2)}, u32[]{:S(2)}) collective-permute-start(f32[32,384]{1,0:T(8,128)S(1)} %reshape.54), channel_id=1, source_target_pairs={{0,128},{128,0},{1,129},{129,1},{2,130},{130,2},{3,131},{131,3},{4... | collective-permute-start | bytes 147464 | tf_op jit(solution)/shard_map/ppermute | solution.py:44
  (17 other events, 195.2 us)
